TPU v7x, 256 devices: a whole 4x4x8 slice. The times are simulated.
256 devices in a mesh: ctx: 64 (over x_hi, y, z), head: 4 (over x_lo, core).
Axes of the slice: x: 4 (x_hi: 2, x_lo: 2; x = x_hi * 2 + x_lo), y: 4, z: 8, core: 2. Of those that a mesh axis runs over, the one named last changes fastest.
Arguments:
- queries: bfloat16 [16384, 6144], P(('ctx', 'head')), may hold values from -42 to 42
- key_head_columns: bfloat16 [16384, 512], P(('ctx', 'head')), may hold values from -4 to 4
- value_head_columns: bfloat16 [16384, 512], P(('ctx', 'head')), may hold values from -6 to 6
- output_gradient: bfloat16 [16384, 6144], P(('ctx', 'head')), may hold values from -6 to 6
- file_starts: int32 [33], replicated, may hold values from 0 to 16320, as said below
- file_imports: int32 [33, 4], replicated, may hold values from -1 to 32, as said below
- header_lens: int32 [33], replicated, may hold values from 16 to 64
Outputs:
- grad_queries: float32 [16384, 6144], P(('ctx', 'head'))
- key_gradient: float32 [16384, 512], P(('ctx', 'head'))
- value_gradient: float32 [16384, 512], P(('ctx', 'head'))
Inputs may be any that keep to these rules, and one draw needn't show every extreme that they name: `file_starts`: Increasing; the first is 0 and the last is 16320; each is a multiple of 64; no two lie in the same aligned block of 256 tokens; each file has 64 tokens or more. `file_imports`: each row lists distinct files other than its own, then -1 in the unused places; file 0 imports nothing.
All inputs are finite; a program needn't handle non-finite values.
Results may differ from a plain program's by a relative error of at most 0.004.
Values may be sent and summed in bfloat16 or wider, within the bound.
A program may use at most 64 MiB of HBM per device.

v0:
```python
import math
import jax
import jax.numpy as jnp
from jax import lax
from jax.sharding import Mesh
from jax.sharding import PartitionSpec as P

WIN = 1024
HDR = 64
HEAD = ("head_0", "head_1")
CTX = ("ctx_0", "ctx_1", "ctx_2")
CTX_HEAD = ("ctx_0", "ctx_1", "ctx_2", "head_0", "head_1")


def in_blocks(array, dim, devices):
    before, after = (array.shape[:dim], array.shape[dim + 1 :])
    return jnp.moveaxis(array.reshape(*before, devices, -1, *after), dim, 0)


def joined_along(parts, dim):
    dims = list(parts.shape[1:])
    dims[dim] *= parts.shape[0]
    return jnp.moveaxis(parts, 0, dim).reshape(dims)


def exchange_in_order(parts, axes, turns):
    dims = [lax.axis_size(a) for a in axes]
    parts = parts.reshape(*dims, *parts.shape[1:])
    for k in turns:
        parts = lax.all_to_all(parts, axes[k], split_axis=k, concat_axis=k, tiled=True)
    return parts.reshape(-1, *parts.shape[len(axes) :])


def two_step_exchange(array, groups, turns, split_dim, concat_dim):
    devices = lax.axis_size(groups[0]) * lax.axis_size(groups[1])
    parts = in_blocks(array, split_dim, devices)
    return joined_along(exchange_in_order(parts, groups, turns), concat_dim)


def passed_along(value, axis, steps):
    count = lax.axis_size(axis)
    first, last = (max(0, -steps), min(count, count - steps))
    return lax.ppermute(value, axis, [(source, source + steps) for source in range(first, last)])


def stacked_from(array, axes, turns):
    parts = array[None]
    for k in turns:
        parts = lax.all_gather(parts, axes[k], axis=0, tiled=True)
    carried = [lax.axis_size(axes[k]) for k in reversed(turns)]
    parts = parts.reshape(*carried, *array.shape)
    turned = sorted(range(len(turns)), key=lambda place: turns[len(turns) - 1 - place])
    return parts.transpose(*turned, *range(len(turns), parts.ndim)).reshape(-1, *array.shape)


def gather_axes(array, axes, turns, dim):
    return joined_along(stacked_from(array, axes, turns), dim)


def own_block(parts, axes, turns):
    inside = parts.shape[1:]
    parts = parts.reshape(*(lax.axis_size(a) for a in axes), *inside)
    parts = jnp.moveaxis(parts, turns, range(len(axes))).reshape(-1, *inside)
    for k in turns:
        parts = lax.psum_scatter(parts, axes[k], scatter_dimension=0, tiled=True)
    return parts[0]


def sum_by_axis(array, axes, turns, dim):
    devices = lax.axis_size(axes)
    return own_block(in_blocks(array, dim, devices), axes, turns)


def local_files(file_starts, file_imports, header_lens, offset_base, span_rows):
    places = offset_base + jnp.arange(span_rows, dtype=jnp.int32)
    before = file_starts[None, :] <= places[:, None]
    file_of = jnp.sum(before.astype(jnp.int32), axis=1) - 1
    file_begin = jnp.max(jnp.where(before, file_starts[None, :], 0), axis=1)
    lower_file = file_of[0]
    upper_file = file_of[span_rows - 1]
    per_file = file_imports.shape[1]
    lower_list = lax.dynamic_slice_in_dim(file_imports, lower_file, 1, 0)[0]
    upper_list = lax.dynamic_slice_in_dim(file_imports, upper_file, 1, 0)[0]
    targets = jnp.concatenate([lower_list, upper_list])
    source_file = jnp.concatenate(
        [jnp.full((per_file,), lower_file, jnp.int32), jnp.full((per_file,), upper_file, jnp.int32)]
    )
    usable = (targets >= 0) & (
        (jnp.arange(2 * per_file, dtype=jnp.int32) < per_file) | (upper_file != lower_file)
    )
    matches = jnp.arange(file_starts.shape[0], dtype=jnp.int32)[None, :] == targets[:, None]
    target_start = jnp.sum(jnp.where(matches, file_starts[None, :], 0), axis=1)
    target_len = jnp.sum(jnp.where(matches, header_lens[None, :], 0), axis=1)
    return (places, file_of, file_begin, source_file, usable, target_start, target_len)


def visibility(places, file_of, file_begin, key_places, source_file, usable, target_len):
    window_ok = (
        (key_places[None, :] <= places[:, None])
        & (key_places[None, :] > places[:, None] - WIN)
        & (key_places[None, :] >= file_begin[:, None])
    )
    offsets = jnp.arange(usable.shape[0] * HDR, dtype=jnp.int32) % HDR
    header_ok = jnp.repeat(usable, HDR) & (offsets < jnp.repeat(target_len, HDR))
    header_vis = header_ok[None, :] & (file_of[:, None] == jnp.repeat(source_file, HDR)[None, :])
    return jnp.concatenate([window_ok, header_vis], axis=1)


def per_device(
    queries,
    key_head_columns,
    value_head_columns,
    output_gradient,
    file_starts,
    file_imports,
    header_lens,
):
    query_rows, key_rows, value_rows, grad_rows = (
        two_step_exchange(queries, ("head_0", "head_1"), (1, 0), 1, 0),
        two_step_exchange(key_head_columns, ("head_0", "head_1"), (1, 0), 1, 0),
        two_step_exchange(value_head_columns, ("head_0", "head_1"), (1, 0), 1, 0),
        two_step_exchange(output_gradient, ("head_0", "head_1"), (1, 0), 1, 0),
    )
    tokens_here = key_rows.shape[0]
    head_size = key_rows.shape[1]
    queries_per_group = query_rows.shape[1] // head_size
    shard_index = lax.axis_index(CTX)
    ctx_count = lax.axis_size(CTX)
    offset_base = shard_index * tokens_here
    scaling = 1.0 / math.sqrt(head_size)
    reach = WIN // tokens_here
    places, file_of, file_begin, source_file, usable, target_start, target_len = local_files(
        file_starts, file_imports, header_lens, offset_base, tokens_here
    )
    block_count = source_file.shape[0]
    stacked = jnp.concatenate([key_rows, value_rows], axis=1)
    earlier = []
    moving = stacked
    for distance in range(1, reach + 1):
        moving = passed_along(moving, CTX, 1)
        earlier.append(moving)
    inside = (file_starts >= offset_base) & (file_starts < offset_base + tokens_here)
    own_offset = jnp.sum(jnp.where(inside, file_starts - offset_base, 0))
    own_header = lax.dynamic_slice_in_dim(stacked, own_offset, HDR, 0)
    all_headers = gather_axes(own_header, CTX, (0, 2, 1), 0)
    header_rows = jnp.concatenate(
        [
            lax.dynamic_slice_in_dim(all_headers, target_start[index] // tokens_here * HDR, HDR, 0)
            for index in range(block_count)
        ],
        axis=0,
    )
    key_table = jnp.concatenate(earlier[::-1] + [stacked, header_rows], axis=0)
    key_matrix = key_table[:, :head_size]
    value_matrix = key_table[:, head_size:]
    window_len = (reach + 1) * tokens_here
    key_places = offset_base - reach * tokens_here + jnp.arange(window_len, dtype=jnp.int32)
    visible = visibility(places, file_of, file_begin, key_places, source_file, usable, target_len)
    heads_block = max(
        (
            divisor
            for divisor in range(1, queries_per_group + 1)
            if queries_per_group % divisor == 0 and divisor * tokens_here <= max(512, tokens_here)
        )
    )
    block_total = queries_per_group // heads_block
    query_blocks = (
        query_rows.reshape(tokens_here, queries_per_group, head_size)
        .transpose(1, 0, 2)
        .reshape(block_total, heads_block, tokens_here, head_size)
    )
    grad_blocks = (
        grad_rows.reshape(tokens_here, queries_per_group, head_size)
        .transpose(1, 0, 2)
        .reshape(block_total, heads_block, tokens_here, head_size)
    )

    def attend(carry, inputs):
        key_gradient_sum, value_gradient_sum = carry
        query_block, grad_block = inputs
        scores = (
            jnp.einsum("htd,kd->htk", query_block, key_matrix, preferred_element_type=jnp.float32)
            * scaling
        )
        scores = jnp.where(visible[None], scores, -jnp.inf)
        ceiling = jnp.max(scores, axis=-1, keepdims=True)
        log_total = ceiling + jnp.log(jnp.sum(jnp.exp(scores - ceiling), axis=-1, keepdims=True))
        weights = jnp.exp(scores - log_total)
        grad_weights = jnp.einsum(
            "htd,kd->htk", grad_block, value_matrix, preferred_element_type=jnp.float32
        )
        centre = jnp.sum(weights * grad_weights, axis=-1, keepdims=True)
        grad_scores = (weights * (grad_weights - centre)).astype(jnp.bfloat16)
        weights_low = weights.astype(jnp.bfloat16)
        grad_query = (
            jnp.einsum("htk,kd->htd", grad_scores, key_matrix, preferred_element_type=jnp.float32)
            * scaling
        )
        key_gradient_sum = (
            key_gradient_sum
            + jnp.einsum(
                "htk,htd->kd", grad_scores, query_block, preferred_element_type=jnp.float32
            )
            * scaling
        )
        value_gradient_sum = value_gradient_sum + jnp.einsum(
            "htk,htd->kd", weights_low, grad_block, preferred_element_type=jnp.float32
        )
        return ((key_gradient_sum, value_gradient_sum), grad_query)

    empty_gradient = jnp.zeros((key_table.shape[0], head_size), jnp.float32)
    (key_gradient_sum, value_gradient_sum), grad_query = lax.scan(
        attend, (empty_gradient, empty_gradient), (query_blocks, grad_blocks)
    )
    grad_query = (
        grad_query.reshape(queries_per_group, tokens_here, head_size)
        .transpose(1, 0, 2)
        .reshape(tokens_here, queries_per_group * head_size)
    )
    combined = jnp.concatenate([key_gradient_sum, value_gradient_sum], axis=1)

    def window_part(index):
        return combined[index * tokens_here : (index + 1) * tokens_here]

    collected = window_part(reach)
    carried = window_part(0)
    for distance in range(1, reach + 1):
        carried = passed_along(carried, CTX, -1)
        if distance < reach:
            carried = carried + window_part(distance)
    collected = collected + carried
    header_part = combined[window_len:]
    slot_table = jnp.zeros((ctx_count * HDR, 2 * head_size), jnp.float32)
    for index in range(block_count):
        at_row = target_start[index] // tokens_here * HDR
        current = lax.dynamic_slice_in_dim(slot_table, at_row, HDR, 0)
        slot_table = lax.dynamic_update_slice_in_dim(
            slot_table, current + header_part[index * HDR : (index + 1) * HDR], at_row, 0
        )
    arriving = sum_by_axis(slot_table, CTX, (1, 2, 0), 0)
    current = lax.dynamic_slice_in_dim(collected, own_offset, HDR, 0)
    collected = lax.dynamic_update_slice_in_dim(collected, current + arriving, own_offset, 0)
    grad_queries, key_gradient, value_gradient = (
        lax.all_to_all(grad_query, HEAD, split_axis=0, concat_axis=1, tiled=True),
        lax.all_to_all(collected[:, :head_size], HEAD, split_axis=0, concat_axis=1, tiled=True),
        lax.all_to_all(collected[:, head_size:], HEAD, split_axis=0, concat_axis=1, tiled=True),
    )
    return (grad_queries, key_gradient, value_gradient)


def solution(mesh):
    split = Mesh(
        mesh.devices.reshape(2, 4, 8, 2, 2), ("ctx_0", "ctx_1", "ctx_2", "head_0", "head_1")
    )
    placed = (
        P(CTX_HEAD, None),
        P(CTX_HEAD, None),
        P(CTX_HEAD, None),
        P(CTX_HEAD, None),
        P(),
        P(),
        P(),
    )
    return jax.shard_map(
        per_device,
        mesh=split,
        in_specs=placed,
        out_specs=(P(CTX_HEAD, None), P(CTX_HEAD, None), P(CTX_HEAD, None)),
        check_vma=False,
    )
```

profile of v0, /device:TPU:1, one launch (start us, length us, event | category | flops | bytes accessed | tf_op | source)
XLA Modules:
  0.0 381.8 jit_solution(10581533873204575703)
XLA Ops:
  8.7 6.5 %all-to-all-start.4 = ((bf16[2,2,64,128]{3,2,0,1:T(8,128)(2,1)}), bf16[2,2,64,128]{3,2,0,1:T(8,128)(2,1)S(1)}, u32[]{:S(2)}, u32[]{:S(2)}) async-start(bf16[2,2,64,128]{3,2,0,1:T(8,128)(2,1)} %copy.125), calls=%async_computation.4 | async-start | bytes 131072 | tf_op jit(solution)/shard_map/all_to_all | solution.py:30
  16.7 3.3 all-to-all-start.2
  21.1 3.3 all-to-all-start.5
  25.0 2.3 all-to-all-done.5
  27.3 3.3 all-to-all-start.3
  30.7 1.3 fusion.41
  34.0 4.9 %all-gather = bf16[128,256]{1,0:T(8,128)(2,1)S(1)} all-gather(bf16[64,256]{1,0:T(8,128)(2,1)S(1)} %fusion.33), channel_id=2, replica_groups=mesh['ctx_0'=2,'ctx_1'=4,'ctx_2'=8,'head_0'=2,'head_1'=2] {'ctx_0'}, dimensions={0}, use_global_device_ids=true | all-gather | bytes 98304 | tf_op jit(solution)/shard_map/all_gather | solution.py:49
  38.9 23.3 %all_gather.10 = bf16[16,64,256]{2,1,0:T(8,128)(2,1)} all-gather(bf16[2,64,256]{2,1,0:T(8,128)(2,1)S(1)} %bitcast.156), channel_id=1, replica_groups=mesh['ctx_0'=2,'ctx_1'=4,'ctx_2'=8,'head_0'=2,'head_1'=2] {'ctx_2'}, dimensions={0}, use_global_device_ids=true | all-gather | bytes 589824 | tf_op jit(solution)/shard_map/all_gather | solution.py:49
  62.2 2.3 reshape.122
  65.6 13.0 %all-to-all-start.6 = ((bf16[2,2,64,1536]{3,2,0,1:T(8,128)(2,1)}), bf16[2,2,64,1536]{3,2,0,1:T(8,128)(2,1)S(1)}, u32[]{:S(2)}, u32[]{:S(2)}) async-start(bf16[2,2,64,1536]{3,2,0,1:T(8,128)(2,1)} %copy.129), calls=%async_computation.6 | async-start | bytes 1572864 | tf_op jit(solution)/shard_map/all_to_all | solution.py:30
  86.2 3.6 all-to-all-start
  91.5 2.6 collective-permute-start
  94.2 3.6 all-to-all-start.7
  121.9 2.6 collective-permute-start.1
  124.6 2.6 collective-permute-done.1
  127.1 4.1 %collective-permute-start.2 = (bf16[256,256]{1,0:T(8,128)(2,1)S(1)}, bf16[256,256]{1,0:T(8,128)(2,1)S(1)}, u32[]{:S(2)}, u32[]{:S(2)}) collective-permute-start(bf16[256,256]{1,0:T(8,128)(2,1)S(1)} %collective-permute-done.1), channel_id=1, source_target_pairs={{0,4},{4,8},{8,12},{12,16},{16,20},{20,24},{24,28},{28,32},{32,36}... | collective-permute-start | bytes 393224 | tf_op jit(solution)/shard_map/ppermute | solution.py:43
  131.2 4.3 %all-to-all-start.1 = ((bf16[2,2,64,1536]{3,2,1,0:T(8,128)(2,1)}), bf16[2,2,64,1536]{3,2,1,0:T(8,128)(2,1)}, u32[]{:S(2)}, u32[]{:S(2)}) async-start(bf16[2,2,64,1536]{3,2,1,0:T(8,128)(2,1)} %copy.119), calls=%async_computation.1 | async-start | bytes 1572864 | tf_op jit(solution)/shard_map/all_to_all | solution.py:30
  135.8 2.8 collective-permute-start.3
  138.6 1.5 reshape_reshape_reshape.7
  140.2 1.4 copy.131
  141.6 3.5 all-to-all-done.1
  145.1 2.4 reshape_reshape_reshape.6
  147.4 2.3 copy.120
  153.1 1.7 copy.127
  160.9 67.9 %while.15 = (s32[]{:T(128)}, f32[1792,128]{1,0:T(8,128)S(1)}, f32[1792,128]{1,0:T(8,128)}, f32[6,2,256,128]{3,2,1,0:T(8,128)}, pred[256,1792]{1,0:T(8,128)(4,1)S...) while((s32[]{:T(128)}, f32[1792,128]{1,0:T(8,128)S(1)}, ...), condition=%wide.region_9.10_spmd.clone, body=%wide.region_5.9_spmd.clone.sunk | while | flops 1188461568 | bytes 80503144 | solution.py:212
  161.0 2.0 fusion.67
  165.6 1.4 fusion.70
  166.9 2.1 fusion.68
  169.0 2.9 fusion.69
  172.0 2.0 fusion.67
  176.6 1.4 fusion.70
  178.0 2.1 fusion.68
  180.1 3.3 fusion.69
  183.4 2.0 fusion.67
  188.0 1.4 fusion.70
  189.3 2.1 fusion.68
  191.5 3.3 fusion.69
  194.8 2.0 fusion.67
  199.4 1.4 fusion.70
  200.7 2.1 fusion.68
  202.8 3.3 fusion.69
  206.1 2.0 fusion.67
  210.7 1.4 fusion.70
  212.1 2.1 fusion.68
  214.2 3.3 fusion.69
  217.5 2.0 fusion.67
  222.1 1.4 fusion.70
  223.5 2.1 fusion.68
  225.6 3.3 fusion.69
  230.7 2.3 copy.134
  233.0 56.0 %reduce-scatter.4.cloned.1.call-done = f32[16,64,256]{2,1,0:T(8,128)} async-done(((f32[64,64,256]{2,1,0:T(8,128)}), f32[16,64,256]{2,1,0:T(8,128)}) %reduce-scatter.4.cloned.1.call-update) | async-done | bytes 1048592 | tf_op jit(solution)/shard_map/reduce_scatter | solution.py:65
  290.4 7.8 %collective-permute-done.4 = f32[256,256]{1,0:T(8,128)S(1)} collective-permute-done((f32[256,256]{1,0:T(8,128)S(1)}, f32[256,256]{1,0:T(8,128)S(1)}, u32[]{:S(2)}, u32[]{:S(2)}) %collective-permute-start.4) | collective-permute-done | bytes 262176 | tf_op jit(solution)/shard_map/ppermute | solution.py:43
  299.6 8.4 %collective-permute-done.5 = f32[256,256]{1,0:T(8,128)S(1)} collective-permute-done((f32[256,256]{1,0:T(8,128)S(1)}, f32[256,256]{1,0:T(8,128)S(1)}, u32[]{:S(2)}, u32[]{:S(2)}) %collective-permute-start.5) | collective-permute-done | bytes 262176 | tf_op jit(solution)/shard_map/ppermute | solution.py:43
  308.0 1.3 collective-permute-start.6
  309.3 2.4 copy.149
  311.7 1.4 all_to_all.74
  313.1 7.4 %all-to-all-start.8 = ((f32[4,64,1536]{2,1,0:T(8,128)}), f32[4,64,1536]{2,1,0:T(8,128)S(1)}, u32[]{:S(2)}, u32[]{:S(2)}) async-start(f32[4,64,1536]{2,1,0:T(8,128)} %all_to_all.74), calls=%async_computation.8 | async-start | bytes 3145728 | tf_op jit(solution)/shard_map/all_to_all | solution.py:244
  322.8 4.6 %reduce-scatter.6.cloned.1.call-done = f32[2,64,256]{2,1,0:T(8,128)} async-done(((f32[16,64,256]{2,1,0:T(8,128)}), f32[2,64,256]{2,1,0:T(8,128)}) %reduce-scatter.6.cloned.1.call-update) | async-done | bytes 131088 | tf_op jit(solution)/shard_map/reduce_scatter | solution.py:65
  327.4 4.0 %collective-permute-done.7 = f32[256,256]{1,0:T(8,128)S(1)} collective-permute-done((f32[256,256]{1,0:T(8,128)S(1)}, f32[256,256]{1,0:T(8,128)S(1)}, u32[]{:S(2)}, u32[]{:S(2)}) %collective-permute-start.7) | collective-permute-done | bytes 262176 | tf_op jit(solution)/shard_map/ppermute | solution.py:43
  332.4 24.7 %reduce-scatter.8.cloned.1.call-done = f32[1,64,256]{2,1,0:T(8,128)} async-done(((f32[2,64,256]{2,1,0:T(8,128)}), f32[1,64,256]{2,1,0:T(8,128)}) %reduce-scatter.8.cloned.1.call-update) | async-done | bytes 65552 | tf_op jit(solution)/shard_map/reduce_scatter | solution.py:65
  359.3 3.8 all-to-all-start.10
  364.3 2.3 all-to-all-done.10
  366.6 4.3 %all-to-all-start.9 = ((f32[4,64,128]{2,1,0:T(8,128)}), f32[4,64,128]{2,1,0:T(8,128)S(1)}, u32[]{:S(2)}, u32[]{:S(2)}) async-start(f32[4,64,128]{2,1,0:T(8,128)} %bitcast.35), calls=%async_computation.12 | async-start | bytes 262144 | tf_op jit(solution)/shard_map/all_to_all | solution.py:245
  371.6 2.9 all-to-all-done.9
  (228 shorter events, 51.2 us)
Async XLA Ops:
  8.7 8.0 %all-to-all-start.4 = ((bf16[2,2,64,128]{3,2,0,1:T(8,128)(2,1)}), bf16[2,2,64,128]{3,2,0,1:T(8,128)(2,1)S(1)}, u32[]{:S(2)}, u32[]{:S(2)}) async-start(bf16[2,2,64,128]{3,2,0,1:T(8,128)(2,1)} %copy.125), calls=%async_computation.4 | async-start | bytes 131072 | tf_op jit(solution)/shard_map/all_to_all | solution.py:30
  16.7 4.4 %all-to-all-start.2 = ((bf16[2,2,64,128]{3,2,0,1:T(8,128)(2,1)}), bf16[2,2,64,128]{3,2,0,1:T(8,128)(2,1)S(1)}, u32[]{:S(2)}, u32[]{:S(2)}) async-start(bf16[2,2,64,128]{3,2,0,1:T(8,128)(2,1)} %copy.122), calls=%async_computation.2 | async-start | bytes 131072 | tf_op jit(solution)/shard_map/all_to_all | solution.py:30
  21.1 6.3 %all-to-all-start.5 = ((bf16[2,2,64,128]{3,2,1,0:T(8,128)(2,1)}), bf16[2,2,64,128]{3,2,1,0:T(8,128)(2,1)S(1)}, u32[]{:S(2)}, u32[]{:S(2)}) async-start(bf16[2,2,64,128]{3,2,1,0:T(8,128)(2,1)} %copy.126), calls=%async_computation.5 | async-start | bytes 131072 | tf_op jit(solution)/shard_map/all_to_all | solution.py:30
  27.3 6.6 %all-to-all-start.3 = ((bf16[2,2,64,128]{3,2,1,0:T(8,128)(2,1)}), bf16[2,2,64,128]{3,2,1,0:T(8,128)(2,1)S(1)}, u32[]{:S(2)}, u32[]{:S(2)}) async-start(bf16[2,2,64,128]{3,2,1,0:T(8,128)(2,1)} %copy.123), calls=%async_computation.3 | async-start | bytes 131072 | tf_op jit(solution)/shard_map/all_to_all | solution.py:30
  30.6 122.4 %all-gather.3.cloned.1.call-start = ((), (), s32[]{:S(2)}) async-start(), calls=%async_computation.14 | async-start | bytes 2621440 | tf_op jit(solution)/shard_map/all_gather | solution.py:49
  38.9 39.8 %copy-start.11 = (s32[33]{0:T(128)S(1)}, s32[33]{0:T(128)}, u32[]{:S(2)}) copy-start(s32[33]{0:T(128)} %param.13) | copy-start | bytes 400
  38.9 44.3 %copy-start.9 = (bf16[64,6144]{1,0:T(8,128)(2,1)S(1)}, bf16[64,6144]{1,0:T(8,128)(2,1)}, u32[]{:S(2)}) copy-start(bf16[64,6144]{1,0:T(8,128)(2,1)} %param.9) | copy-start | bytes 2359300
  65.6 20.6 %all-to-all-start.6 = ((bf16[2,2,64,1536]{3,2,0,1:T(8,128)(2,1)}), bf16[2,2,64,1536]{3,2,0,1:T(8,128)(2,1)S(1)}, u32[]{:S(2)}, u32[]{:S(2)}) async-start(bf16[2,2,64,1536]{3,2,0,1:T(8,128)(2,1)} %copy.129), calls=%async_computation.6 | async-start | bytes 1572864 | tf_op jit(solution)/shard_map/all_to_all | solution.py:30
  83.2 7.5 %copy-start.10 = (s32[33,4]{0,1:T(4,128)S(1)}, s32[33,4]{0,1:T(4,128)}, u32[]{:S(2)}) copy-start(s32[33,4]{0,1:T(4,128)} %param.14) | copy-start | bytes 1588
  83.9 13.8 %copy-start.12 = (s32[33]{0:T(128)S(1)}, s32[33]{0:T(128)}, u32[]{:S(2)}) copy-start(s32[33]{0:T(128)} %param.15) | copy-start | bytes 400
  86.2 8.0 %all-to-all-start = ((bf16[2,2,64,1536]{3,2,0,1:T(8,128)(2,1)}), bf16[2,2,64,1536]{3,2,0,1:T(8,128)(2,1)S(1)}, u32[]{:S(2)}, u32[]{:S(2)}) async-start(bf16[2,2,64,1536]{3,2,0,1:T(8,128)(2,1)} %copy.118), calls=%async_computation | async-start | bytes 1572864 | tf_op jit(solution)/shard_map/all_to_all | solution.py:30
  91.5 30.4 %collective-permute-start = (bf16[256,256]{1,0:T(8,128)(2,1)S(1)}, bf16[256,256]{1,0:T(8,128)(2,1)S(1)}, u32[]{:S(2)}, u32[]{:S(2)}) collective-permute-start(bf16[256,256]{1,0:T(8,128)(2,1)S(1)} %pad_maximum_fusion), channel_id=1, source_target_pairs={{0,4},{4,8},{8,12},{12,16},{16,20},{20,24},{24,28},{28,32},{32,36}... | collective-permute-start | bytes 393224 | tf_op jit(solution)/shard_map/ppermute | solution.py:43
  94.2 37.1 %all-to-all-start.7 = ((bf16[2,2,64,1536]{3,2,1,0:T(8,128)(2,1)}), bf16[2,2,64,1536]{3,2,1,0:T(8,128)(2,1)S(1)}, u32[]{:S(2)}, u32[]{:S(2)}) async-start(bf16[2,2,64,1536]{3,2,1,0:T(8,128)(2,1)} %copy.130), calls=%async_computation.7 | async-start | bytes 1572864 | tf_op jit(solution)/shard_map/all_to_all | solution.py:30
  121.9 5.2 %collective-permute-start.1 = (bf16[256,256]{1,0:T(8,128)(2,1)S(1)}, bf16[256,256]{1,0:T(8,128)(2,1)S(1)}, u32[]{:S(2)}, u32[]{:S(2)}) collective-permute-start(bf16[256,256]{1,0:T(8,128)(2,1)S(1)} %collective-permute-done), channel_id=1, source_target_pairs={{0,4},{4,8},{8,12},{12,16},{16,20},{20,24},{24,28},{28,32},{32,36}... | collective-permute-start | bytes 393224 | tf_op jit(solution)/shard_map/ppermute | solution.py:43
  127.1 8.7 %collective-permute-start.2 = (bf16[256,256]{1,0:T(8,128)(2,1)S(1)}, bf16[256,256]{1,0:T(8,128)(2,1)S(1)}, u32[]{:S(2)}, u32[]{:S(2)}) collective-permute-start(bf16[256,256]{1,0:T(8,128)(2,1)S(1)} %collective-permute-done.1), channel_id=1, source_target_pairs={{0,4},{4,8},{8,12},{12,16},{16,20},{20,24},{24,28},{28,32},{32,36}... | collective-permute-start | bytes 393224 | tf_op jit(solution)/shard_map/ppermute | solution.py:43
  131.2 13.8 %all-to-all-start.1 = ((bf16[2,2,64,1536]{3,2,1,0:T(8,128)(2,1)}), bf16[2,2,64,1536]{3,2,1,0:T(8,128)(2,1)}, u32[]{:S(2)}, u32[]{:S(2)}) async-start(bf16[2,2,64,1536]{3,2,1,0:T(8,128)(2,1)} %copy.119), calls=%async_computation.1 | async-start | bytes 1572864 | tf_op jit(solution)/shard_map/all_to_all | solution.py:30
  135.5 153.5 %reduce-scatter.4.cloned.1.call-start = ((), (), s32[]{:S(2)}) async-start(), calls=%async_computation.15 | async-start | bytes 5242880 | tf_op jit(solution)/shard_map/reduce_scatter | solution.py:65
  135.8 14.0 %collective-permute-start.3 = (bf16[256,256]{1,0:T(8,128)(2,1)S(1)}, bf16[256,256]{1,0:T(8,128)(2,1)S(1)}, u32[]{:S(2)}, u32[]{:S(2)}) collective-permute-start(bf16[256,256]{1,0:T(8,128)(2,1)S(1)} %collective-permute-done.2), channel_id=1, source_target_pairs={{0,4},{4,8},{8,12},{12,16},{16,20},{20,24},{24,28},{28,32},{32,36}... | collective-permute-start | bytes 393224 | tf_op jit(solution)/shard_map/ppermute | solution.py:43
  160.9 2.7 copy-start.2
  161.0 2.7 copy-start.4
  161.0 3.6 copy-start.6
  169.0 3.0 copy-start.3
  169.0 3.0 copy-start.5
  169.0 3.0 copy-start.7
  172.0 2.7 copy-start.2
  172.0 2.7 copy-start.4
  172.0 3.6 copy-start.6
  180.0 3.3 copy-start.3
  180.1 3.3 copy-start.5
  180.1 3.3 copy-start.7
  183.4 2.7 copy-start.2
  183.4 2.7 copy-start.4
  183.4 3.6 copy-start.6
  191.4 3.3 copy-start.3
  191.4 3.3 copy-start.5
  191.4 3.3 copy-start.7
  194.7 2.7 copy-start.2
  194.7 2.7 copy-start.4
  194.8 3.6 copy-start.6
  202.8 3.3 copy-start.3
  202.8 3.3 copy-start.5
  202.8 3.3 copy-start.7
  206.1 2.7 copy-start.2
  206.1 2.7 copy-start.4
  206.1 3.6 copy-start.6
  214.2 3.3 copy-start.3
  214.2 3.3 copy-start.5
  214.2 3.3 copy-start.7
  217.5 2.7 copy-start.2
  217.5 2.7 copy-start.4
  217.5 3.6 copy-start.6
  225.5 3.3 copy-start.3
  225.6 3.3 copy-start.5
  225.6 3.3 copy-start.7
  230.2 77.8 %copy-start.8 = (f32[1792,256]{1,0:T(8,128)}, f32[1792,256]{1,0:T(8,128)S(1)}, u32[]{:S(2)}) copy-start(f32[1792,256]{1,0:T(8,128)S(1)} %constant_dynamic-update-slice_fusion.13) | copy-start | bytes 5505028
  233.0 94.4 %reduce-scatter.6.cloned.1.call-start = ((), (), s32[]{:S(2)}) async-start(), calls=%async_computation.16 | async-start | bytes 1179648 | tf_op jit(solution)/shard_map/reduce_scatter | solution.py:65
  289.1 9.1 %collective-permute-start.4 = (f32[256,256]{1,0:T(8,128)S(1)}, f32[256,256]{1,0:T(8,128)S(1)}, u32[]{:S(2)}, u32[]{:S(2)}) collective-permute-start(f32[256,256]{1,0:T(8,128)S(1)} %slice.128), channel_id=1, source_target_pairs={{4,0},{8,4},{12,8},{16,12},{20,16},{24,20},{28,24},{32,28},{36,32}... | collective-permute-start | bytes 786440 | tf_op jit(solution)/shard_map/ppermute | solution.py:43
  298.3 9.7 %collective-permute-start.5 = (f32[256,256]{1,0:T(8,128)S(1)}, f32[256,256]{1,0:T(8,128)S(1)}, u32[]{:S(2)}, u32[]{:S(2)}) collective-permute-start(f32[256,256]{1,0:T(8,128)S(1)} %slice_add_fusion.2), channel_id=1, source_target_pairs={{4,0},{8,4},{12,8},{16,12},{20,16},{24,20},{28,24},{32,28},{36,32}... | collective-permute-start | bytes 786440 | tf_op jit(solution)/shard_map/ppermute | solution.py:43
  308.0 12.5 %collective-permute-start.6 = (f32[256,256]{1,0:T(8,128)S(1)}, f32[256,256]{1,0:T(8,128)S(1)}, u32[]{:S(2)}, u32[]{:S(2)}) collective-permute-start(f32[256,256]{1,0:T(8,128)S(1)} %slice_add_fusion.1), channel_id=1, source_target_pairs={{4,0},{8,4},{12,8},{16,12},{20,16},{24,20},{28,24},{32,28},{36,32}... | collective-permute-start | bytes 786440 | tf_op jit(solution)/shard_map/ppermute | solution.py:43
  313.1 46.2 %all-to-all-start.8 = ((f32[4,64,1536]{2,1,0:T(8,128)}), f32[4,64,1536]{2,1,0:T(8,128)S(1)}, u32[]{:S(2)}, u32[]{:S(2)}) async-start(f32[4,64,1536]{2,1,0:T(8,128)} %all_to_all.74), calls=%async_computation.8 | async-start | bytes 3145728 | tf_op jit(solution)/shard_map/all_to_all | solution.py:244
  320.5 36.6 %reduce-scatter.8.cloned.1.call-start = ((), (), s32[]{:S(2)}) async-start(), calls=%async_computation.17 | async-start | bytes 196608 | tf_op jit(solution)/shard_map/reduce_scatter | solution.py:65
  321.5 9.9 %collective-permute-start.7 = (f32[256,256]{1,0:T(8,128)S(1)}, f32[256,256]{1,0:T(8,128)S(1)}, u32[]{:S(2)}, u32[]{:S(2)}) collective-permute-start(f32[256,256]{1,0:T(8,128)S(1)} %slice_add_fusion), channel_id=1, source_target_pairs={{4,0},{8,4},{12,8},{16,12},{20,16},{24,20},{28,24},{32,28},{36,32}... | collective-permute-start | bytes 786440 | tf_op jit(solution)/shard_map/ppermute | solution.py:43
  359.3 7.4 %all-to-all-start.10 = ((f32[4,64,128]{2,1,0:T(8,128)}), f32[4,64,128]{2,1,0:T(8,128)S(1)}, u32[]{:S(2)}, u32[]{:S(2)}) async-start(f32[4,64,128]{2,1,0:T(8,128)} %bitcast.37), calls=%async_computation.13 | async-start | bytes 262144 | tf_op jit(solution)/shard_map/all_to_all | solution.py:246
  366.6 7.9 %all-to-all-start.9 = ((f32[4,64,128]{2,1,0:T(8,128)}), f32[4,64,128]{2,1,0:T(8,128)S(1)}, u32[]{:S(2)}, u32[]{:S(2)}) async-start(f32[4,64,128]{2,1,0:T(8,128)} %bitcast.35), calls=%async_computation.12 | async-start | bytes 262144 | tf_op jit(solution)/shard_map/all_to_all | solution.py:245
  (12 other events, 23.4 us)
Sparse Core Ops, SparseCore 0:
  62.3 41.5 all-gather.2
  233.1 55.9 reduce-scatter.3
  291.8 35.5 reduce-scatter.5
  329.8 27.2 reduce-scatter.7
where the time goes:
time: 384 us; the launch traced here: 382 us
  waiting for transfers between devices  120 us (31%)
  starting transfers between devices  73.9 us (19%)
  matrix products  57.4 us (15%)
  local copies, waits for them, and re-layouts  45.2 us (12%)
  between operations  41.9 us (11%)
  blocking collectives  28.2 us (7%)
  other arithmetic  14.8 us (4%)
    reduce_scatter x3, waiting for transfers between devices, own_block(): parts = lax.psum_scatter(parts, axes[k], scatter_dimension=0, tiled=True)  85.3 us
    all_to_all x8, starting transfers between devices, exchange_in_order(): lax.all_to_all(parts, axes[k], split_axis=k, concat_axis=k, tiled=True)  40.9 us
    all_gather x2, blocking collectives, stacked_from(): parts = lax.all_gather(parts, axes[k], axis=0, tiled=True)  28.2 us
    ppermute x8, waiting for transfers between devices, passed_along(): lax.ppermute(value, axis, [(source, source + steps) for source in range(f...  22.9 us
    dot_general x6, matrix products, attend(): jnp.einsum('htk,htd->kd', weights_low, grad_block, preferred_element_type...  19.2 us
    ppermute x8, starting transfers between devices, passed_along(): lax.ppermute(value, axis, [(source, source + steps) for source in range(f...  17.3 us
    dot_general x6, matrix products, attend(): jnp.einsum('htk,htd->kd', grad_scores, query_block, preferred_element_typ...  12.5 us
    dot_general x6, matrix products, attend(): jnp.einsum('htd,kd->htk', query_block, key_matrix, preferred_element_type...  11.9 us
  transfers between devices with their start and end apart: 23, of which 12 were waited for; matrix products, arithmetic and copies ran while one was open for 9% of the time, Pallas kernels for 0%

commit v1 on v0

--- a/solution.py
+++ b/solution.py
@@ -46,7 +46,9 @@
 def stacked_from(array, axes, turns):
     parts = array[None]
     for k in turns:
-        parts = lax.all_gather(parts, axes[k], axis=0, tiled=True)
+        parts = jnp.concatenate(
+            lax.all_to_all(jnp.stack([parts] * lax.axis_size(axes[k])), axes[k], 0, 0), axis=0
+        )
     carried = [lax.axis_size(axes[k]) for k in reversed(turns)]
     parts = parts.reshape(*carried, *array.shape)
     turned = sorted(range(len(turns)), key=lambda place: turns[len(turns) - 1 - place])

time: 384 us -> 399 us (1.039)
  waiting for transfers between devices: 120 us -> 154 us
  blocking collectives: 28.2 us -> 4.35 us
    all_gather x2 -> x0, blocking collectives: 28.2 us -> none  [stacked_from(): parts = lax.all_gather(parts, axes[k], axis=0, tiled=True)]
    all_to_all x8 -> x7, waiting for transfers between devices: 6.21 us -> 21 us  [exchange_in_order(): lax.all_to_all(parts, axes[k], split_axis=k, concat_axis=k, tiled=True)]
    all_to_all x0 -> x3, starting transfers between devices: none -> 13.6 us  [stacked_from(): lax.all_to_all(jnp.stack([parts] * lax.axis_size(axes[k])), axes[k], 0, 0)]
    all_to_all x8 -> x7, starting transfers between devices: 40.9 us -> 28.5 us  [exchange_in_order(): lax.all_to_all(parts, axes[k], split_axis=k, concat_axis=k, tiled=True)]
    all_to_all x0 -> x3, waiting for transfers between devices: none -> 10.1 us  [stacked_from(): lax.all_to_all(jnp.stack([parts] * lax.axis_size(axes[k])), axes[k], 0, 0)]
    reduce_scatter x3, waiting for transfers between devices: 85.3 us -> 92.9 us  [own_block(): parts = lax.psum_scatter(parts, axes[k], scatter_dimension=0, tiled=True)]
    all_to_all x0 -> x1, blocking collectives: none -> 4.35 us  [exchange_in_order(): lax.all_to_all(parts, axes[k], split_axis=k, concat_axis=k, tiled=True)]
  transfers between devices with their start and end apart: 23 -> 24, of which waited for: 12 -> 17; matrix products, arithmetic and copies ran while one was open for 9% -> 9% of each run, Pallas kernels for 0% -> 0%
where the time goes in v1:
time: 399 us; the launch traced here: 396 us
  waiting for transfers between devices  154 us (39%)
  starting transfers between devices  75.3 us (19%)
  matrix products  57.5 us (14%)
  local copies, waits for them, and re-layouts  47.4 us (12%)
  between operations  41.3 us (10%)
  other arithmetic  15.4 us (4%)
  blocking collectives  4.35 us (1%)
    reduce_scatter x3, waiting for transfers between devices, own_block(): parts = lax.psum_scatter(parts, axes[k], scatter_dimension=0, tiled=True)  92.9 us
    all_to_all x7, starting transfers between devices, exchange_in_order(): lax.all_to_all(parts, axes[k], split_axis=k, concat_axis=k, tiled=True)  28.5 us
    ppermute x8, waiting for transfers between devices, passed_along(): lax.ppermute(value, axis, [(source, source + steps) for source in range(f...  25 us
    all_to_all x7, waiting for transfers between devices, exchange_in_order(): lax.all_to_all(parts, axes[k], split_axis=k, concat_axis=k, tiled=True)  21 us
    dot_general x6, matrix products, attend(): jnp.einsum('htk,htd->kd', weights_low, grad_block, preferred_element_type...  19.4 us
    ppermute x8, starting transfers between devices, passed_along(): lax.ppermute(value, axis, [(source, source + steps) for source in range(f...  17.6 us
    all_to_all x3, starting transfers between devices, stacked_from(): lax.all_to_all(jnp.stack([parts] * lax.axis_size(axes[k])), axes[k], 0, 0)  13.6 us
    dot_general x6, matrix products, attend(): jnp.einsum('htk,htd->kd', grad_scores, query_block, preferred_element_typ...  12.5 us
  transfers between devices with their start and end apart: 24, of which 17 were waited for; matrix products, arithmetic and copies ran while one was open for 9% of the time, Pallas kernels for 0%

profile of v1, /device:TPU:1, one launch (start us, length us, event | category | flops | bytes accessed | tf_op | source)
XLA Modules:
  0.0 396.3 jit_solution(12572855513388957938)
XLA Ops:
  8.7 6.5 %all-to-all-start.4 = ((bf16[2,2,64,128]{3,2,0,1:T(8,128)(2,1)}), bf16[2,2,64,128]{3,2,0,1:T(8,128)(2,1)S(1)}, u32[]{:S(2)}, u32[]{:S(2)}) async-start(bf16[2,2,64,128]{3,2,0,1:T(8,128)(2,1)} %copy.125), calls=%async_computation.4 | async-start | bytes 131072 | tf_op jit(solution)/shard_map/all_to_all | solution.py:30
  16.8 3.3 all-to-all-start.2
  21.2 3.3 all-to-all-start.5
  25.1 2.3 all-to-all-done.5
  27.4 3.3 all-to-all-start.3
  33.3 2.3 reshape.122
  38.2 5.0 %all-to-all-start.9 = ((bf16[2,2,64,1536]{3,2,0,1:T(8,128)(2,1)}), bf16[2,2,64,1536]{3,2,0,1:T(8,128)(2,1)S(1)}, u32[]{:S(2)}, u32[]{:S(2)}) async-start(bf16[2,2,64,1536]{3,2,0,1:T(8,128)(2,1)} %copy.129), calls=%async_computation.9 | async-start | bytes 1572864 | tf_op jit(solution)/shard_map/all_to_all | solution.py:30
  44.8 4.4 %all_to_all.112 = bf16[2,2,64,1536]{3,2,0,1:T(8,128)(2,1)S(1)} all-to-all(bf16[2,2,64,1536]{3,2,0,1:T(8,128)(2,1)S(1)} %copy.118), channel_id=1, replica_groups=mesh['ctx_0'=2,'ctx_1'=4,'ctx_2'=8,'head_0'=2,'head_1'=2] {'head_1'}, dimensions={1} | all-to-all | bytes 1572864 | tf_op jit(solution)/shard_map/all_to_all | solution.py:30
  49.1 3.3 all-to-all-start.6
  53.4 3.5 all-to-all-done.6
  56.9 3.5 all-to-all-start.10
  61.4 8.9 %all-to-all-done.10 = bf16[2,2,64,1536]{3,2,1,0:T(8,128)(2,1)S(1)} async-done(((bf16[2,2,64,1536]{3,2,1,0:T(8,128)(2,1)}), bf16[2,2,64,1536]{3,2,1,0:T(8,128)(2,1)S(1)}, u32[]{:S(2)}, u32[]{:S(2)}) %all-to-all-start.10) | async-done | bytes 786464 | tf_op jit(solution)/shard_map/all_to_all | solution.py:30
  70.2 3.5 all-to-all-start.1
  73.9 8.5 %all-to-all-done.1 = bf16[2,2,64,1536]{3,2,1,0:T(8,128)(2,1)S(1)} async-done(((bf16[2,2,64,1536]{3,2,1,0:T(8,128)(2,1)}), bf16[2,2,64,1536]{3,2,1,0:T(8,128)(2,1)S(1)}, u32[]{:S(2)}, u32[]{:S(2)}) %all-to-all-start.1) | async-done | bytes 786464 | tf_op jit(solution)/shard_map/all_to_all | solution.py:30
  83.3 5.8 %all-to-all-start.7 = ((bf16[8,2,64,256]{3,2,1,0:T(8,128)(2,1)}), bf16[8,2,64,256]{3,2,1,0:T(8,128)(2,1)S(1)}, u32[]{:S(2)}, u32[]{:S(2)}) async-start(bf16[8,2,64,256]{3,2,1,0:T(8,128)(2,1)} %stack.10), calls=%async_computation.7 | async-start | bytes 1048576 | tf_op jit(solution)/shard_map/all_to_all | solution.py:50
  95.6 6.7 %all-to-all-done.7 = bf16[8,2,64,256]{3,2,1,0:T(8,128)(2,1)S(1)} async-done(((bf16[8,2,64,256]{3,2,1,0:T(8,128)(2,1)}), bf16[8,2,64,256]{3,2,1,0:T(8,128)(2,1)S(1)}, u32[]{:S(2)}, u32[]{:S(2)}) %all-to-all-start.7) | async-done | bytes 524320 | tf_op jit(solution)/shard_map/all_to_all | solution.py:50
  102.2 1.6 stack.11
  103.8 4.5 %all-to-all-start.8 = ((bf16[4,16,64,256]{3,2,1,0:T(8,128)(2,1)}), bf16[4,16,64,256]{3,2,1,0:T(8,128)(2,1)}, u32[]{:S(2)}, u32[]{:S(2)}) async-start(bf16[4,16,64,256]{3,2,1,0:T(8,128)(2,1)} %stack.11), calls=%async_computation.8 | async-start | bytes 4194304 | tf_op jit(solution)/shard_map/all_to_all | solution.py:50
  108.4 1.6 collective-permute-start
  132.6 3.1 collective-permute-start.1
  135.7 1.9 collective-permute-done.1
  137.6 3.8 collective-permute-start.2
  141.6 2.6 collective-permute-done.2
  144.2 4.0 %collective-permute-start.3 = (bf16[256,256]{1,0:T(8,128)(2,1)S(1)}, bf16[256,256]{1,0:T(8,128)(2,1)S(1)}, u32[]{:S(2)}, u32[]{:S(2)}) collective-permute-start(bf16[256,256]{1,0:T(8,128)(2,1)S(1)} %collective-permute-done.2), channel_id=1, source_target_pairs={{0,4},{4,8},{8,12},{12,16},{16,20},{20,24},{24,28},{28,32},{32,36}... | collective-permute-start | bytes 393224 | tf_op jit(solution)/shard_map/ppermute | solution.py:43
  148.3 1.5 reshape_reshape_reshape.7
  149.8 1.4 copy.131
  151.2 2.4 reshape_reshape_reshape.6
  153.6 2.3 copy.120
  159.3 1.7 copy.127
  167.2 68.4 %while.15 = (s32[]{:T(128)}, f32[1792,128]{1,0:T(8,128)S(1)}, f32[1792,128]{1,0:T(8,128)}, f32[6,2,256,128]{3,2,1,0:T(8,128)}, pred[256,1792]{1,0:T(8,128)(4,1)S...) while((s32[]{:T(128)}, f32[1792,128]{1,0:T(8,128)S(1)}, ...), condition=%wide.region_9.10_spmd.clone, body=%wide.region_5.9_spmd.clone.sunk | while | flops 1188461568 | bytes 80503144 | solution.py:214
  167.2 2.0 fusion.68
  173.2 2.1 fusion.69
  175.3 2.9 fusion.70
  178.3 2.0 fusion.68
  183.0 1.4 fusion.71
  184.3 2.1 fusion.69
  186.5 3.3 fusion.70
  189.8 2.0 fusion.68
  195.8 2.1 fusion.69
  197.9 3.3 fusion.70
  201.3 2.0 fusion.68
  207.3 2.1 fusion.69
  209.4 3.3 fusion.70
  212.7 2.0 fusion.68
  217.4 1.4 fusion.71
  218.7 2.1 fusion.69
  220.9 3.3 fusion.70
  224.2 2.0 fusion.68
  230.2 2.1 fusion.69
  232.3 3.3 fusion.70
  237.4 2.3 copy.134
  239.8 63.8 %reduce-scatter.4.cloned.1.call-done = f32[16,64,256]{2,1,0:T(8,128)} async-done(((f32[64,64,256]{2,1,0:T(8,128)}), f32[16,64,256]{2,1,0:T(8,128)}) %reduce-scatter.4.cloned.1.call-update) | async-done | bytes 1048592 | tf_op jit(solution)/shard_map/reduce_scatter | solution.py:67
  305.0 7.8 %collective-permute-done.4 = f32[256,256]{1,0:T(8,128)S(1)} collective-permute-done((f32[256,256]{1,0:T(8,128)S(1)}, f32[256,256]{1,0:T(8,128)S(1)}, u32[]{:S(2)}, u32[]{:S(2)}) %collective-permute-start.4) | collective-permute-done | bytes 262176 | tf_op jit(solution)/shard_map/ppermute | solution.py:43
  314.2 8.4 %collective-permute-done.5 = f32[256,256]{1,0:T(8,128)S(1)} collective-permute-done((f32[256,256]{1,0:T(8,128)S(1)}, f32[256,256]{1,0:T(8,128)S(1)}, u32[]{:S(2)}, u32[]{:S(2)}) %collective-permute-start.5) | collective-permute-done | bytes 262176 | tf_op jit(solution)/shard_map/ppermute | solution.py:43
  323.9 2.4 copy.149
  326.3 1.4 all_to_all.86
  327.7 7.4 %all-to-all-start.11 = ((f32[4,64,1536]{2,1,0:T(8,128)}), f32[4,64,1536]{2,1,0:T(8,128)S(1)}, u32[]{:S(2)}, u32[]{:S(2)}) async-start(f32[4,64,1536]{2,1,0:T(8,128)} %all_to_all.86), calls=%async_computation.11 | async-start | bytes 3145728 | tf_op jit(solution)/shard_map/all_to_all | solution.py:246
  337.4 4.7 %reduce-scatter.6.cloned.1.call-done = f32[2,64,256]{2,1,0:T(8,128)} async-done(((f32[16,64,256]{2,1,0:T(8,128)}), f32[2,64,256]{2,1,0:T(8,128)}) %reduce-scatter.6.cloned.1.call-update) | async-done | bytes 131088 | tf_op jit(solution)/shard_map/reduce_scatter | solution.py:67
  342.1 4.2 %collective-permute-done.7 = f32[256,256]{1,0:T(8,128)S(1)} collective-permute-done((f32[256,256]{1,0:T(8,128)S(1)}, f32[256,256]{1,0:T(8,128)S(1)}, u32[]{:S(2)}, u32[]{:S(2)}) %collective-permute-start.7) | collective-permute-done | bytes 262176 | tf_op jit(solution)/shard_map/ppermute | solution.py:43
  347.2 24.5 %reduce-scatter.8.cloned.1.call-done = f32[1,64,256]{2,1,0:T(8,128)} async-done(((f32[2,64,256]{2,1,0:T(8,128)}), f32[1,64,256]{2,1,0:T(8,128)}) %reduce-scatter.8.cloned.1.call-update) | async-done | bytes 65552 | tf_op jit(solution)/shard_map/reduce_scatter | solution.py:67
  373.8 3.8 all-to-all-start.13
  378.9 2.3 all-to-all-done.13
  381.2 4.3 %all-to-all-start.12 = ((f32[4,64,128]{2,1,0:T(8,128)}), f32[4,64,128]{2,1,0:T(8,128)S(1)}, u32[]{:S(2)}, u32[]{:S(2)}) async-start(f32[4,64,128]{2,1,0:T(8,128)} %bitcast.37), calls=%async_computation.15 | async-start | bytes 262144 | tf_op jit(solution)/shard_map/all_to_all | solution.py:247
  386.2 2.9 all-to-all-done.12
  (233 shorter events, 61.1 us)
Async XLA Ops:
  7.2 29.6 %copy-start.10 = (bf16[64,6144]{1,0:T(8,128)(2,1)S(1)}, bf16[64,6144]{1,0:T(8,128)(2,1)}, u32[]{:S(2)}) copy-start(bf16[64,6144]{1,0:T(8,128)(2,1)} %param.9) | copy-start | bytes 2359300
  8.7 8.0 %all-to-all-start.4 = ((bf16[2,2,64,128]{3,2,0,1:T(8,128)(2,1)}), bf16[2,2,64,128]{3,2,0,1:T(8,128)(2,1)S(1)}, u32[]{:S(2)}, u32[]{:S(2)}) async-start(bf16[2,2,64,128]{3,2,0,1:T(8,128)(2,1)} %copy.125), calls=%async_computation.4 | async-start | bytes 131072 | tf_op jit(solution)/shard_map/all_to_all | solution.py:30
  16.8 4.4 %all-to-all-start.2 = ((bf16[2,2,64,128]{3,2,0,1:T(8,128)(2,1)}), bf16[2,2,64,128]{3,2,0,1:T(8,128)(2,1)S(1)}, u32[]{:S(2)}, u32[]{:S(2)}) async-start(bf16[2,2,64,128]{3,2,0,1:T(8,128)(2,1)} %copy.122), calls=%async_computation.2 | async-start | bytes 131072 | tf_op jit(solution)/shard_map/all_to_all | solution.py:30
  21.2 6.3 %all-to-all-start.5 = ((bf16[2,2,64,128]{3,2,1,0:T(8,128)(2,1)}), bf16[2,2,64,128]{3,2,1,0:T(8,128)(2,1)S(1)}, u32[]{:S(2)}, u32[]{:S(2)}) async-start(bf16[2,2,64,128]{3,2,1,0:T(8,128)(2,1)} %copy.126), calls=%async_computation.5 | async-start | bytes 131072 | tf_op jit(solution)/shard_map/all_to_all | solution.py:30
  27.4 10.7 %all-to-all-start.3 = ((bf16[2,2,64,128]{3,2,1,0:T(8,128)(2,1)}), bf16[2,2,64,128]{3,2,1,0:T(8,128)(2,1)S(1)}, u32[]{:S(2)}, u32[]{:S(2)}) async-start(bf16[2,2,64,128]{3,2,1,0:T(8,128)(2,1)} %copy.123), calls=%async_computation.3 | async-start | bytes 131072 | tf_op jit(solution)/shard_map/all_to_all | solution.py:30
  38.2 6.6 %all-to-all-start.9 = ((bf16[2,2,64,1536]{3,2,0,1:T(8,128)(2,1)}), bf16[2,2,64,1536]{3,2,0,1:T(8,128)(2,1)S(1)}, u32[]{:S(2)}, u32[]{:S(2)}) async-start(bf16[2,2,64,1536]{3,2,0,1:T(8,128)(2,1)} %copy.129), calls=%async_computation.9 | async-start | bytes 1572864 | tf_op jit(solution)/shard_map/all_to_all | solution.py:30
  43.9 29.9 %copy-start.12 = (s32[33]{0:T(128)S(1)}, s32[33]{0:T(128)}, u32[]{:S(2)}) copy-start(s32[33]{0:T(128)} %param.13) | copy-start | bytes 400
  49.1 7.8 %all-to-all-start.6 = ((bf16[2,1,64,256]{3,2,1,0:T(8,128)(2,1)}), bf16[2,1,64,256]{3,2,1,0:T(8,128)(2,1)S(1)}, u32[]{:S(2)}, u32[]{:S(2)}) async-start(bf16[2,1,64,256]{3,2,1,0:T(8,128)(2,1)} %pad_maximum_fusion.1), calls=%async_computation.6 | async-start | bytes 131072 | tf_op jit(solution)/shard_map/all_to_all | solution.py:50
  52.4 42.4 %copy-start.11 = (s32[33,4]{0,1:T(4,128)S(1)}, s32[33,4]{0,1:T(4,128)}, u32[]{:S(2)}) copy-start(s32[33,4]{0,1:T(4,128)} %param.14) | copy-start | bytes 1588
  56.9 13.3 %all-to-all-start.10 = ((bf16[2,2,64,1536]{3,2,1,0:T(8,128)(2,1)}), bf16[2,2,64,1536]{3,2,1,0:T(8,128)(2,1)S(1)}, u32[]{:S(2)}, u32[]{:S(2)}) async-start(bf16[2,2,64,1536]{3,2,1,0:T(8,128)(2,1)} %copy.130), calls=%async_computation.10 | async-start | bytes 1572864 | tf_op jit(solution)/shard_map/all_to_all | solution.py:30
  70.2 12.2 %all-to-all-start.1 = ((bf16[2,2,64,1536]{3,2,1,0:T(8,128)(2,1)}), bf16[2,2,64,1536]{3,2,1,0:T(8,128)(2,1)S(1)}, u32[]{:S(2)}, u32[]{:S(2)}) async-start(bf16[2,2,64,1536]{3,2,1,0:T(8,128)(2,1)} %copy.119), calls=%async_computation.1 | async-start | bytes 1572864 | tf_op jit(solution)/shard_map/all_to_all | solution.py:30
  82.4 21.4 %copy-start.9 = (bf16[2,2,64,1536]{3,2,1,0:T(8,128)(2,1)}, bf16[2,2,64,1536]{3,2,1,0:T(8,128)(2,1)S(1)}, u32[]{:S(2)}) copy-start(bf16[2,2,64,1536]{3,2,1,0:T(8,128)(2,1)S(1)} %all-to-all-done.1) | copy-start | bytes 2359300
  83.3 19.0 %all-to-all-start.7 = ((bf16[8,2,64,256]{3,2,1,0:T(8,128)(2,1)}), bf16[8,2,64,256]{3,2,1,0:T(8,128)(2,1)S(1)}, u32[]{:S(2)}, u32[]{:S(2)}) async-start(bf16[8,2,64,256]{3,2,1,0:T(8,128)(2,1)} %stack.10), calls=%async_computation.7 | async-start | bytes 1048576 | tf_op jit(solution)/shard_map/all_to_all | solution.py:50
  95.1 14.8 %copy-start.13 = (s32[33]{0:T(128)S(1)}, s32[33]{0:T(128)}, u32[]{:S(2)}) copy-start(s32[33]{0:T(128)} %param.15) | copy-start | bytes 400
  103.8 55.5 %all-to-all-start.8 = ((bf16[4,16,64,256]{3,2,1,0:T(8,128)(2,1)}), bf16[4,16,64,256]{3,2,1,0:T(8,128)(2,1)}, u32[]{:S(2)}, u32[]{:S(2)}) async-start(bf16[4,16,64,256]{3,2,1,0:T(8,128)(2,1)} %stack.11), calls=%async_computation.8 | async-start | bytes 4194304 | tf_op jit(solution)/shard_map/all_to_all | solution.py:50
  108.3 195.4 %reduce-scatter.4.cloned.1.call-start = ((), (), s32[]{:S(2)}) async-start(), calls=%async_computation.17 | async-start | bytes 5242880 | tf_op jit(solution)/shard_map/reduce_scatter | solution.py:67
  108.4 24.2 %collective-permute-start = (bf16[256,256]{1,0:T(8,128)(2,1)S(1)}, bf16[256,256]{1,0:T(8,128)(2,1)S(1)}, u32[]{:S(2)}, u32[]{:S(2)}) collective-permute-start(bf16[256,256]{1,0:T(8,128)(2,1)S(1)} %pad_maximum_fusion), channel_id=1, source_target_pairs={{0,4},{4,8},{8,12},{12,16},{16,20},{20,24},{24,28},{28,32},{32,36}... | collective-permute-start | bytes 393224 | tf_op jit(solution)/shard_map/ppermute | solution.py:43
  132.6 5.0 %collective-permute-start.1 = (bf16[256,256]{1,0:T(8,128)(2,1)S(1)}, bf16[256,256]{1,0:T(8,128)(2,1)S(1)}, u32[]{:S(2)}, u32[]{:S(2)}) collective-permute-start(bf16[256,256]{1,0:T(8,128)(2,1)S(1)} %collective-permute-done), channel_id=1, source_target_pairs={{0,4},{4,8},{8,12},{12,16},{16,20},{20,24},{24,28},{28,32},{32,36}... | collective-permute-start | bytes 393224 | tf_op jit(solution)/shard_map/ppermute | solution.py:43
  137.6 6.6 %collective-permute-start.2 = (bf16[256,256]{1,0:T(8,128)(2,1)S(1)}, bf16[256,256]{1,0:T(8,128)(2,1)S(1)}, u32[]{:S(2)}, u32[]{:S(2)}) collective-permute-start(bf16[256,256]{1,0:T(8,128)(2,1)S(1)} %collective-permute-done.1), channel_id=1, source_target_pairs={{0,4},{4,8},{8,12},{12,16},{16,20},{20,24},{24,28},{28,32},{32,36}... | collective-permute-start | bytes 393224 | tf_op jit(solution)/shard_map/ppermute | solution.py:43
  144.2 11.7 %collective-permute-start.3 = (bf16[256,256]{1,0:T(8,128)(2,1)S(1)}, bf16[256,256]{1,0:T(8,128)(2,1)S(1)}, u32[]{:S(2)}, u32[]{:S(2)}) collective-permute-start(bf16[256,256]{1,0:T(8,128)(2,1)S(1)} %collective-permute-done.2), channel_id=1, source_target_pairs={{0,4},{4,8},{8,12},{12,16},{16,20},{20,24},{24,28},{28,32},{32,36}... | collective-permute-start | bytes 393224 | tf_op jit(solution)/shard_map/ppermute | solution.py:43
  167.2 2.7 copy-start.2
  167.2 2.7 copy-start.4
  167.2 3.6 copy-start.6
  175.3 3.0 copy-start.3
  175.3 3.0 copy-start.5
  175.3 3.0 copy-start.7
  178.3 2.7 copy-start.2
  178.3 2.7 copy-start.4
  178.3 3.6 copy-start.6
  186.4 3.3 copy-start.3
  186.4 3.3 copy-start.5
  186.4 3.3 copy-start.7
  189.8 2.7 copy-start.2
  189.8 2.7 copy-start.4
  189.8 3.6 copy-start.6
  197.9 3.3 copy-start.3
  197.9 3.3 copy-start.5
  197.9 3.3 copy-start.7
  201.2 2.7 copy-start.4
  201.3 3.6 copy-start.6
  209.4 3.3 copy-start.3
  209.4 3.3 copy-start.5
  209.4 3.3 copy-start.7
  212.7 2.7 copy-start.2
  212.7 2.7 copy-start.4
  212.7 3.6 copy-start.6
  220.8 3.3 copy-start.3
  220.8 3.3 copy-start.5
  220.8 3.3 copy-start.7
  224.2 2.7 copy-start.4
  224.2 3.6 copy-start.6
  232.3 3.3 copy-start.3
  232.3 3.3 copy-start.5
  232.3 3.3 copy-start.7
  236.9 85.7 %copy-start.8 = (f32[1792,256]{1,0:T(8,128)}, f32[1792,256]{1,0:T(8,128)S(1)}, u32[]{:S(2)}) copy-start(f32[1792,256]{1,0:T(8,128)S(1)} %constant_dynamic-update-slice_fusion.13) | copy-start | bytes 5505028
  239.8 102.3 %reduce-scatter.6.cloned.1.call-start = ((), (), s32[]{:S(2)}) async-start(), calls=%async_computation.18 | async-start | bytes 1179648 | tf_op jit(solution)/shard_map/reduce_scatter | solution.py:67
  303.7 9.1 %collective-permute-start.4 = (f32[256,256]{1,0:T(8,128)S(1)}, f32[256,256]{1,0:T(8,128)S(1)}, u32[]{:S(2)}, u32[]{:S(2)}) collective-permute-start(f32[256,256]{1,0:T(8,128)S(1)} %slice.128), channel_id=1, source_target_pairs={{4,0},{8,4},{12,8},{16,12},{20,16},{24,20},{28,24},{32,28},{36,32}... | collective-permute-start | bytes 786440 | tf_op jit(solution)/shard_map/ppermute | solution.py:43
  312.9 9.7 %collective-permute-start.5 = (f32[256,256]{1,0:T(8,128)S(1)}, f32[256,256]{1,0:T(8,128)S(1)}, u32[]{:S(2)}, u32[]{:S(2)}) collective-permute-start(f32[256,256]{1,0:T(8,128)S(1)} %slice_add_fusion.2), channel_id=1, source_target_pairs={{4,0},{8,4},{12,8},{16,12},{20,16},{24,20},{28,24},{32,28},{36,32}... | collective-permute-start | bytes 786440 | tf_op jit(solution)/shard_map/ppermute | solution.py:43
  322.6 12.5 %collective-permute-start.6 = (f32[256,256]{1,0:T(8,128)S(1)}, f32[256,256]{1,0:T(8,128)S(1)}, u32[]{:S(2)}, u32[]{:S(2)}) collective-permute-start(f32[256,256]{1,0:T(8,128)S(1)} %slice_add_fusion.1), channel_id=1, source_target_pairs={{4,0},{8,4},{12,8},{16,12},{20,16},{24,20},{28,24},{32,28},{36,32}... | collective-permute-start | bytes 786440 | tf_op jit(solution)/shard_map/ppermute | solution.py:43
  327.7 46.1 %all-to-all-start.11 = ((f32[4,64,1536]{2,1,0:T(8,128)}), f32[4,64,1536]{2,1,0:T(8,128)S(1)}, u32[]{:S(2)}, u32[]{:S(2)}) async-start(f32[4,64,1536]{2,1,0:T(8,128)} %all_to_all.86), calls=%async_computation.11 | async-start | bytes 3145728 | tf_op jit(solution)/shard_map/all_to_all | solution.py:246
  335.1 36.6 %reduce-scatter.8.cloned.1.call-start = ((), (), s32[]{:S(2)}) async-start(), calls=%async_computation.19 | async-start | bytes 196608 | tf_op jit(solution)/shard_map/reduce_scatter | solution.py:67
  336.1 10.2 %collective-permute-start.7 = (f32[256,256]{1,0:T(8,128)S(1)}, f32[256,256]{1,0:T(8,128)S(1)}, u32[]{:S(2)}, u32[]{:S(2)}) collective-permute-start(f32[256,256]{1,0:T(8,128)S(1)} %slice_add_fusion), channel_id=1, source_target_pairs={{4,0},{8,4},{12,8},{16,12},{20,16},{24,20},{28,24},{32,28},{36,32}... | collective-permute-start | bytes 786440 | tf_op jit(solution)/shard_map/ppermute | solution.py:43
  373.8 7.4 %all-to-all-start.13 = ((f32[4,64,128]{2,1,0:T(8,128)}), f32[4,64,128]{2,1,0:T(8,128)S(1)}, u32[]{:S(2)}, u32[]{:S(2)}) async-start(f32[4,64,128]{2,1,0:T(8,128)} %bitcast.39), calls=%async_computation.16 | async-start | bytes 262144 | tf_op jit(solution)/shard_map/all_to_all | solution.py:248
  381.2 7.9 %all-to-all-start.12 = ((f32[4,64,128]{2,1,0:T(8,128)}), f32[4,64,128]{2,1,0:T(8,128)S(1)}, u32[]{:S(2)}, u32[]{:S(2)}) async-start(f32[4,64,128]{2,1,0:T(8,128)} %bitcast.37), calls=%async_computation.15 | async-start | bytes 262144 | tf_op jit(solution)/shard_map/all_to_all | solution.py:247
  (14 other events, 29.1 us)
Sparse Core Ops, SparseCore 0:
  239.9 63.7 reduce-scatter.3
  306.3 35.6 reduce-scatter.5
  344.7 26.9 reduce-scatter.7
